TPU v7x, 32 devices: a whole 2x2x4 slice. The times are simulated.
32 devices in a mesh: groups: 1, user: 16 (over z, y, x), item: 2 (over core).
Axes of the slice: x: 2, y: 2, z: 4, core: 2. Of those that a mesh axis runs over, the one named last changes fastest.
Arguments:
- blocks: bfloat16 [14336, 16, 256], P(('groups', 'user', 'item')), may hold values from -12 to 12
- user_blocks: int32 [14336], P(('groups', 'user', 'item')), may hold values from 0 to 127, as said below
- item_blocks: int32 [14336], P(('groups', 'user', 'item')), may hold values from 0 to 31, as said below
- time_blocks: int32 [14336], P(('groups', 'user', 'item')), may hold values from 0 to 15
- block_counts: int32 [32], P(('groups', 'user', 'item')), may hold values from 28 to 448, as said below
- item_factor: bfloat16 [512, 256], P(('groups', 'user', 'item')), may hold values from -0.25 to 0.25
- item_previous: bfloat16 [512, 256], P(('groups', 'user', 'item')), may hold values from -0.25 to 0.25
- time_factor: bfloat16 [256, 256], P(('groups', 'user')), may hold values from -0.375 to 0.375
- time_previous: bfloat16 [256, 256], P(('groups', 'user')), may hold values from -0.375 to 0.375
Outputs:
- row_products: float32 [2, 2048, 256], P(None, ('groups', 'user', 'item'))
- hadamard_grams: float32 [2, 256, 256], P('groups')
Inputs may be any that keep to these rules, and one draw needn't show every extreme that they name: `block_counts`: the live slots of a device come first among its 448 slots; some device has 448 of them and another 448 // 16. `user_blocks`: A slot of device d (slot index div 448) names a user block of range d div 2: its index lies from (d div 2) * 64 * 2 // 16 up to one range further. `item_blocks`: A slot of device d names an item block that lies in the item factor rows of some device e with e mod 2 = d mod 2 (rows e * 16 to (e + 1) * 16 - 1).
All inputs are finite; a program needn't handle non-finite values.
Results may differ from a plain program's by a relative error of at most 0.0049.
Values may be sent and summed in bfloat16 or wider, within the bound.
A program may use at most 64 MiB of HBM per device.

v0:
```python
import jax
import jax.numpy as jnp
from jax import lax
from jax.sharding import PartitionSpec as P

R = 256
BS = 16
U_DEV = 64


extrapolation = 0.5


def extended(current, previous):
    wide_now = current.astype(jnp.float32)
    grown = wide_now + extrapolation * (wide_now - previous.astype(jnp.float32))
    return grown.astype(jnp.bfloat16)


def local(
    blocks,
    user_blocks,
    item_blocks,
    time_blocks,
    block_counts,
    item_factor,
    item_previous,
    time_factor,
    time_previous,
):
    live_count = block_counts[0]
    n_item = lax.axis_size("item")
    item_sets = jnp.stack([item_factor, extended(item_factor, item_previous)])
    time_sets = jnp.stack([time_factor, extended(time_factor, time_previous)])
    shard_rows = item_factor.shape[0]
    item_whole = lax.all_gather(item_sets, "user", axis=1, tiled=True)
    time_whole = lax.all_gather(time_sets, "user", axis=1, tiled=True)
    item_tiles = item_whole.reshape(2, -1, BS, R)
    time_tiles = time_whole.reshape(2, -1, BS, R)
    per_shard = shard_rows // BS
    range_rows = U_DEV * n_item
    range_tiles = range_rows // BS
    user_local = user_blocks - lax.axis_index("user") * range_tiles
    item_local = item_blocks // per_shard // n_item * per_shard + item_blocks % per_shard
    slots = blocks.shape[0]
    group = min(32, slots)

    def advance(turn, total):
        start = turn * group
        tensor = lax.dynamic_slice_in_dim(blocks, start, group, 0)
        user_index = lax.dynamic_slice_in_dim(user_local, start, group, 0)
        item_index = lax.dynamic_slice_in_dim(item_local, start, group, 0)
        time_index = lax.dynamic_slice_in_dim(time_blocks, start, group, 0)
        alive = start + jnp.arange(group, dtype=jnp.int32) < live_count
        tensor = jnp.where(alive[:, None, None], tensor, jnp.zeros_like(tensor))
        left = item_tiles[:, item_index].astype(jnp.float32)
        right = time_tiles[:, time_index].astype(jnp.float32)
        khatri = (left[:, :, :, None, :] * right[:, :, None, :, :]).astype(jnp.bfloat16)
        khatri = khatri.reshape(2, group, BS * BS, R)
        part = jnp.einsum("gaq,sgqr->gasr", tensor, khatri, preferred_element_type=jnp.float32)
        return total + jax.ops.segment_sum(part, user_index, num_segments=range_tiles)

    empty = jnp.zeros((range_tiles, BS, 2, R), jnp.float32)
    turns = slots // group
    total = lax.fori_loop(0, turns, advance, empty)
    partial_value = total.reshape(range_rows, 2, R)
    owned = lax.psum_scatter(partial_value, "item", scatter_dimension=0, tiled=True)
    row_products = owned.transpose(1, 0, 2)
    item_own = jnp.einsum("sir,sic->src", item_sets, item_sets, preferred_element_type=jnp.float32)
    time_own = jnp.einsum("sir,sic->src", time_sets, time_sets, preferred_element_type=jnp.float32)
    item_gram = lax.psum(item_own, ("user", "item"))
    time_gram = lax.psum(time_own, "user")
    return (row_products, item_gram * time_gram)


def solution(mesh):
    in_specs = (
        P(("groups", "user", "item"), None, None),
        P(("groups", "user", "item")),
        P(("groups", "user", "item")),
        P(("groups", "user", "item")),
        P(("groups", "user", "item")),
        P(("groups", "user", "item"), None),
        P(("groups", "user", "item"), None),
        P(("groups", "user"), None),
        P(("groups", "user"), None),
    )
    out_specs = (P(None, ("groups", "user", "item"), None), P("groups", None, None))
    return jax.shard_map(local, mesh=mesh, in_specs=in_specs, out_specs=out_specs, check_vma=False)
```

profile of v0, /device:TPU:0, one launch (start us, length us, event | category | flops | bytes accessed | tf_op | source)
XLA Modules:
  0.0 328.6 jit_solution(16051422785829805151)
XLA Ops:
  8.8 1.8 fusion.17
  11.4 1.8 fusion.16
  14.7 46.5 %all_gather.7 = bf16[2,256,256]{2,1,0:T(8,128)(2,1)} all-gather(bf16[2,16,256]{2,1,0:T(8,128)(2,1)S(1)} %pad_maximum_fusion.1), channel_id=1, replica_groups=mesh['groups'=1,'user'=16,'item'=2] {'user'}, dimensions={1}, use_global_device_ids=true | all-gather | bytes 278528 | tf_op jit(solution)/shard_map/all_gather | solution.py:37
  61.2 39.5 %all_gather.6 = bf16[2,256,256]{2,1,0:T(8,128)(2,1)} all-gather(bf16[2,16,256]{2,1,0:T(8,128)(2,1)S(1)} %pad_maximum_fusion), channel_id=1, replica_groups=mesh['groups'=1,'user'=16,'item'=2] {'user'}, dimensions={1}, use_global_device_ids=true | all-gather | bytes 278528 | tf_op jit(solution)/shard_map/all_gather | solution.py:36
  101.4 213.6 %while.13 = (s32[]{:T(128)}, f32[8,16,2,256]{3,1,2,0:T(8,128)S(1)}, s32[448]{0:T(512)S(1)}, s32[]{:T(128)}, bf16[448,16,256]{2,1,0:T(8,128)(2,1)}, /*index=5*/s3...) while((s32[]{:T(128)}, f32[8,16,2,256]{3,1,2,0:T(8,128)S(1)}, ...), condition=%wide.region_2.3_spmd, body=%wide.region_0.2_spmd.sunk | while | flops 143526144 | bytes 28583552 | solution.py:65
  102.2 1.5 gather_fusion
  103.8 1.5 gather_fusion.1
  106.5 5.0 %multiply_convert_fusion.2 = bf16[2,32,16,16,256]{4,3,2,0,1:T(8,128)(2,1)S(1)} fusion(f32[2,32,16,256]{3,2,0,1:T(8,128)S(1)} %convert_bitcast_fusion.4, f32[2,32,16,256]{3,2,0,1:T(8,128)} %convert_bitcast_fusion.5), kind=kLoop, calls=%fused_computation.3.clone.1 | loop fusion | flops 8388608 | bytes 10485760 | tf_op jit(solution)/shard_map/while/body/eval_jaxpr/convert_element_type | solution.py:58
  112.2 2.2 fusion.24
  114.5 2.2 scatter_fusion
  117.4 1.5 gather_fusion
  119.1 1.5 gather_fusion.1
  121.8 5.0 %multiply_convert_fusion.2 = bf16[2,32,16,16,256]{4,3,2,0,1:T(8,128)(2,1)S(1)} fusion(f32[2,32,16,256]{3,2,0,1:T(8,128)S(1)} %convert_bitcast_fusion.4, f32[2,32,16,256]{3,2,0,1:T(8,128)} %convert_bitcast_fusion.5), kind=kLoop, calls=%fused_computation.3.clone.1 | loop fusion | flops 8388608 | bytes 10485760 | tf_op jit(solution)/shard_map/while/body/eval_jaxpr/convert_element_type | solution.py:58
  127.5 2.2 fusion.24
  129.7 2.2 scatter_fusion
  132.7 1.5 gather_fusion
  134.4 1.5 gather_fusion.1
  137.0 5.0 %multiply_convert_fusion.2 = bf16[2,32,16,16,256]{4,3,2,0,1:T(8,128)(2,1)S(1)} fusion(f32[2,32,16,256]{3,2,0,1:T(8,128)S(1)} %convert_bitcast_fusion.4, f32[2,32,16,256]{3,2,0,1:T(8,128)} %convert_bitcast_fusion.5), kind=kLoop, calls=%fused_computation.3.clone.1 | loop fusion | flops 8388608 | bytes 10485760 | tf_op jit(solution)/shard_map/while/body/eval_jaxpr/convert_element_type | solution.py:58
  142.7 2.2 fusion.24
  145.0 2.2 scatter_fusion
  147.9 1.5 gather_fusion
  149.6 1.5 gather_fusion.1
  152.3 5.0 %multiply_convert_fusion.2 = bf16[2,32,16,16,256]{4,3,2,0,1:T(8,128)(2,1)S(1)} fusion(f32[2,32,16,256]{3,2,0,1:T(8,128)S(1)} %convert_bitcast_fusion.4, f32[2,32,16,256]{3,2,0,1:T(8,128)} %convert_bitcast_fusion.5), kind=kLoop, calls=%fused_computation.3.clone.1 | loop fusion | flops 8388608 | bytes 10485760 | tf_op jit(solution)/shard_map/while/body/eval_jaxpr/convert_element_type | solution.py:58
  158.0 2.2 fusion.24
  160.2 2.2 scatter_fusion
  163.2 1.5 gather_fusion
  164.9 1.5 gather_fusion.1
  167.6 5.0 %multiply_convert_fusion.2 = bf16[2,32,16,16,256]{4,3,2,0,1:T(8,128)(2,1)S(1)} fusion(f32[2,32,16,256]{3,2,0,1:T(8,128)S(1)} %convert_bitcast_fusion.4, f32[2,32,16,256]{3,2,0,1:T(8,128)} %convert_bitcast_fusion.5), kind=kLoop, calls=%fused_computation.3.clone.1 | loop fusion | flops 8388608 | bytes 10485760 | tf_op jit(solution)/shard_map/while/body/eval_jaxpr/convert_element_type | solution.py:58
  173.2 2.2 fusion.24
  175.5 2.2 scatter_fusion
  178.5 1.5 gather_fusion
  182.8 5.0 %multiply_convert_fusion.2 = bf16[2,32,16,16,256]{4,3,2,0,1:T(8,128)(2,1)S(1)} fusion(f32[2,32,16,256]{3,2,0,1:T(8,128)S(1)} %convert_bitcast_fusion.4, f32[2,32,16,256]{3,2,0,1:T(8,128)} %convert_bitcast_fusion.5), kind=kLoop, calls=%fused_computation.3.clone.1 | loop fusion | flops 8388608 | bytes 10485760 | tf_op jit(solution)/shard_map/while/body/eval_jaxpr/convert_element_type | solution.py:58
  188.5 2.2 fusion.24
  190.8 2.2 scatter_fusion
  195.4 1.5 gather_fusion.1
  198.1 5.0 %multiply_convert_fusion.2 = bf16[2,32,16,16,256]{4,3,2,0,1:T(8,128)(2,1)S(1)} fusion(f32[2,32,16,256]{3,2,0,1:T(8,128)S(1)} %convert_bitcast_fusion.4, f32[2,32,16,256]{3,2,0,1:T(8,128)} %convert_bitcast_fusion.5), kind=kLoop, calls=%fused_computation.3.clone.1 | loop fusion | flops 8388608 | bytes 10485760 | tf_op jit(solution)/shard_map/while/body/eval_jaxpr/convert_element_type | solution.py:58
  203.8 2.2 fusion.24
  206.0 2.2 scatter_fusion
  209.0 1.5 gather_fusion
  213.3 5.0 %multiply_convert_fusion.2 = bf16[2,32,16,16,256]{4,3,2,0,1:T(8,128)(2,1)S(1)} fusion(f32[2,32,16,256]{3,2,0,1:T(8,128)S(1)} %convert_bitcast_fusion.4, f32[2,32,16,256]{3,2,0,1:T(8,128)} %convert_bitcast_fusion.5), kind=kLoop, calls=%fused_computation.3.clone.1 | loop fusion | flops 8388608 | bytes 10485760 | tf_op jit(solution)/shard_map/while/body/eval_jaxpr/convert_element_type | solution.py:58
  219.0 2.2 fusion.24
  221.3 2.1 scatter_fusion
  224.2 1.5 gather_fusion
  225.9 1.5 gather_fusion.1
  228.6 5.0 %multiply_convert_fusion.2 = bf16[2,32,16,16,256]{4,3,2,0,1:T(8,128)(2,1)S(1)} fusion(f32[2,32,16,256]{3,2,0,1:T(8,128)S(1)} %convert_bitcast_fusion.4, f32[2,32,16,256]{3,2,0,1:T(8,128)} %convert_bitcast_fusion.5), kind=kLoop, calls=%fused_computation.3.clone.1 | loop fusion | flops 8388608 | bytes 10485760 | tf_op jit(solution)/shard_map/while/body/eval_jaxpr/convert_element_type | solution.py:58
  234.3 2.2 fusion.24
  236.5 2.2 scatter_fusion
  243.9 5.0 %multiply_convert_fusion.2 = bf16[2,32,16,16,256]{4,3,2,0,1:T(8,128)(2,1)S(1)} fusion(f32[2,32,16,256]{3,2,0,1:T(8,128)S(1)} %convert_bitcast_fusion.4, f32[2,32,16,256]{3,2,0,1:T(8,128)} %convert_bitcast_fusion.5), kind=kLoop, calls=%fused_computation.3.clone.1 | loop fusion | flops 8388608 | bytes 10485760 | tf_op jit(solution)/shard_map/while/body/eval_jaxpr/convert_element_type | solution.py:58
  249.6 2.2 fusion.24
  251.8 2.2 scatter_fusion
  259.1 5.0 %multiply_convert_fusion.2 = bf16[2,32,16,16,256]{4,3,2,0,1:T(8,128)(2,1)S(1)} fusion(f32[2,32,16,256]{3,2,0,1:T(8,128)S(1)} %convert_bitcast_fusion.4, f32[2,32,16,256]{3,2,0,1:T(8,128)} %convert_bitcast_fusion.5), kind=kLoop, calls=%fused_computation.3.clone.1 | loop fusion | flops 8388608 | bytes 10485760 | tf_op jit(solution)/shard_map/while/body/eval_jaxpr/convert_element_type | solution.py:58
  264.8 2.2 fusion.24
  267.1 2.2 scatter_fusion
  274.4 5.0 %multiply_convert_fusion.2 = bf16[2,32,16,16,256]{4,3,2,0,1:T(8,128)(2,1)S(1)} fusion(f32[2,32,16,256]{3,2,0,1:T(8,128)S(1)} %convert_bitcast_fusion.4, f32[2,32,16,256]{3,2,0,1:T(8,128)} %convert_bitcast_fusion.5), kind=kLoop, calls=%fused_computation.3.clone.1 | loop fusion | flops 8388608 | bytes 10485760 | tf_op jit(solution)/shard_map/while/body/eval_jaxpr/convert_element_type | solution.py:58
  280.1 2.2 fusion.24
  282.3 2.2 scatter_fusion
  289.6 5.0 %multiply_convert_fusion.2 = bf16[2,32,16,16,256]{4,3,2,0,1:T(8,128)(2,1)S(1)} fusion(f32[2,32,16,256]{3,2,0,1:T(8,128)S(1)} %convert_bitcast_fusion.4, f32[2,32,16,256]{3,2,0,1:T(8,128)} %convert_bitcast_fusion.5), kind=kLoop, calls=%fused_computation.3.clone.1 | loop fusion | flops 8388608 | bytes 10485760 | tf_op jit(solution)/shard_map/while/body/eval_jaxpr/convert_element_type | solution.py:58
  295.3 2.2 fusion.24
  297.6 2.2 scatter_fusion
  304.9 5.0 %multiply_convert_fusion.2 = bf16[2,32,16,16,256]{4,3,2,0,1:T(8,128)(2,1)S(1)} fusion(f32[2,32,16,256]{3,2,0,1:T(8,128)S(1)} %convert_bitcast_fusion.4, f32[2,32,16,256]{3,2,0,1:T(8,128)} %convert_bitcast_fusion.5), kind=kLoop, calls=%fused_computation.3.clone.1 | loop fusion | flops 8388608 | bytes 10485760 | tf_op jit(solution)/shard_map/while/body/eval_jaxpr/convert_element_type | solution.py:58
  310.6 2.2 fusion.24
  312.9 2.1 scatter_fusion
  315.8 2.1 mul.57
  317.9 3.3 %reduce-scatter.2.cloned.1.call-done = f32[64,2,256]{2,0,1:T(8,128)} async-done(((f32[128,2,256]{2,0,1:T(8,128)}), f32[64,2,256]{2,0,1:T(8,128)}) %reduce-scatter.2.cloned.1.call-update) | async-done | bytes 131088 | tf_op jit(solution)/shard_map/reduce_scatter | solution.py:67
  (126 shorter events, 63.0 us)
Async XLA Ops:
  8.0 307.8 %all-reduce.3.cloned.1.call-start = ((), (), s32[]{:S(2)}) async-start(), calls=%async_computation.2 | async-start | bytes 1048576 | tf_op jit(solution)/shard_map/psum | solution.py:71
  10.6 305.2 %all-reduce.5.cloned.1.call-start = ((), (), s32[]{:S(2)}) async-start(), calls=%async_computation.3 | async-start | bytes 1048576 | tf_op jit(solution)/shard_map/psum | solution.py:72
  13.3 307.9 %reduce-scatter.2.cloned.1.call-start = ((), (), s32[]{:S(2)}) async-start(), calls=%async_computation.1 | async-start | bytes 393216 | tf_op jit(solution)/shard_map/reduce_scatter | solution.py:67
Sparse Core Ops, SparseCore 0:
  15.5 130.8 all-reduce.2
  151.6 107.3 all-reduce.4
Sparse Core Ops, SparseCore 1:
  315.8 5.3 reduce-scatter.1
where the time goes:
time: 331 us; the launch traced here: 329 us
  other arithmetic  144 us (44%)
  blocking collectives  85.9 us (26%)
  local copies, waits for them, and re-layouts  44.6 us (13%)
  matrix products  34.3 us (10%)
  between operations  15.5 us (5%)
  waiting for transfers between devices  3.39 us (1%)
    convert_element_type x14, other arithmetic, advance(): (left[:, :, :, None, :] * right[:, :, None, :, :]).astype(jnp.bfloat16)  70.4 us
    all_gather x1, blocking collectives, local(): time_whole = lax.all_gather(time_sets, 'user', axis=1, tiled=True)  46.5 us
    all_gather x1, blocking collectives, local(): item_whole = lax.all_gather(item_sets, 'user', axis=1, tiled=True)  39.5 us
    dot_general x14, matrix products, advance(): jnp.einsum('gaq,sgqr->gasr', tensor, khatri, preferred_element_type=jnp.f...  30.6 us
    scatter-add x14, other arithmetic, advance(): jax.ops.segment_sum(part, user_index, num_segments=range_tiles)  30.1 us
    gather x14, local copies, waits for them, and re-layouts, advance(): left = item_tiles[:, item_index].astype(jnp.float32)  21.4 us
    gather x14, local copies, waits for them, and re-layouts, advance(): right = time_tiles[:, time_index].astype(jnp.float32)  21.4 us
    convert_element_type x14, other arithmetic, advance(): left = item_tiles[:, item_index].astype(jnp.float32)  15.9 us
  transfers between devices with their start and end apart: 3, of which 1 were waited for; matrix products, arithmetic and copies ran while one was open for 67% of the time, Pallas kernels for 0%

commit v1 on v0

v1 whole, which is shorter than its diff:
```python
import functools

import jax
import jax.numpy as jnp
from jax import lax
from jax.experimental import pallas as pl
from jax.experimental.pallas import tpu as pltpu
from jax.sharding import PartitionSpec as P

BS = 16
U_DEV = 64
LANE = 128
WIDTH = 4
UNROLL = 4
DEAD = 1 << 28

extrapolation = 0.5


def extended(current, previous):
    wide_now = current.astype(jnp.float32)
    grown = wide_now + extrapolation * (wide_now - previous.astype(jnp.float32))
    return grown.astype(jnp.bfloat16)


def as_columns(row, size):
    parts = []
    for at in range(0, size, LANE):
        square = jnp.broadcast_to(row[:, at : at + LANE], (LANE, LANE))
        parts.append(square.T)
    return jnp.concatenate(parts, axis=0)


def plan_groups(key, value, table_ref):
    size = key.shape[1]
    down = lax.broadcasted_iota(jnp.int32, (size, LANE), 0)
    across = lax.broadcasted_iota(jnp.int32, (1, LANE), 1)
    chunks = [slice(at, at + LANE) for at in range(0, size, LANE)]
    key_col = as_columns(key, size)
    places = []
    for n, cut in enumerate(chunks):
        earlier = (key_col == key[:, cut]) & (down < across + n * LANE)
        places.append(jnp.sum(earlier.astype(jnp.int32), axis=0, keepdims=True))
    place = jnp.concatenate(places, axis=1)
    alive = key < DEAD
    order = jnp.where(alive, key * size + place, jnp.int32(2**31 - 1))
    order_col = as_columns(order, size)
    leads = (order_col & (WIDTH - 1)) == 0
    groups = []
    for cut in chunks:
        ahead = leads & (order_col <= order[:, cut])
        groups.append(jnp.sum(ahead.astype(jnp.int32), axis=0, keepdims=True))
    group = jnp.concatenate(groups, axis=1) - 1
    spot = jnp.where(alive, group * WIDTH + (place & (WIDTH - 1)), -1)
    spot_col = as_columns(spot, size)
    value_col = as_columns(value, size)
    zero = jnp.zeros_like(key_col)
    table_ref[...] = jnp.zeros(table_ref.shape, jnp.int32)
    for n, cut in enumerate(chunks):
        base = (across + n * LANE) * WIDTH
        for m in range(WIDTH):
            here = spot_col == base + m
            picked = jnp.sum(jnp.where(here, value_col, zero), axis=0, keepdims=True)
            table_ref[m : m + 1, cut] = picked
            if m == 0:
                keys = jnp.sum(jnp.where(here, key_col, zero), axis=0, keepdims=True)
                table_ref[WIDTH : WIDTH + 1, cut] = keys
    total = jnp.sum(leads.astype(jnp.int32), axis=0, keepdims=True)
    table_ref[WIDTH + 1 : WIDTH + 2, 0:LANE] = total


def gather_kernel(
    n_user, key_ref, value_ref, item_ref, item_old_ref, time_ref, time_old_ref,
    items_ref, times_ref, table_ref, own, held, send_sem, recv_sem,
):
    me = lax.axis_index("user")
    rows_i, rows_t = item_ref.shape[0], time_ref.shape[0]
    barrier = pltpu.get_barrier_semaphore()

    def greet(d, carry):
        peer = lax.rem(me + d, n_user)
        pl.semaphore_signal(barrier, inc=1, device_id={"user": peer}, device_id_type=pl.DeviceIdType.MESH)
        return carry

    lax.fori_loop(1, n_user, greet, 0)
    own[0:rows_i] = item_ref[...]
    own[rows_i : 2 * rows_i] = extended(item_ref[...], item_old_ref[...])
    own[2 * rows_i : 2 * rows_i + rows_t] = time_ref[...]
    own[2 * rows_i + rows_t :] = extended(time_ref[...], time_old_ref[...])
    pl.semaphore_wait(barrier, n_user - 1)

    def copy(d, slot, peer):
        return pltpu.make_async_remote_copy(
            src_ref=own, dst_ref=held.at[slot], send_sem=send_sem.at[d], recv_sem=recv_sem.at[d],
            device_id={"user": peer}, device_id_type=pl.DeviceIdType.MESH,
        )

    def send(d, carry):
        copy(d, me, lax.rem(me + d, n_user)).start()
        return carry

    lax.fori_loop(1, n_user, send, 0)
    plan_groups(key_ref[...], value_ref[...], table_ref)

    def place(source, block):
        at_i = pl.multiple_of(source * rows_i, rows_i)
        at_t = pl.multiple_of(source * rows_t, rows_t)
        for s in range(2):
            items_ref[s, pl.ds(at_i, rows_i)] = block[s * rows_i : (s + 1) * rows_i]
            low = 2 * rows_i + s * rows_t
            times_ref[s, pl.ds(at_t, rows_t)] = block[low : low + rows_t]

    place(me, own)

    def take(d, carry):
        source = lax.rem(me - d + n_user, n_user)
        copy(d, source, source).wait_recv()
        place(source, held.at[source])
        return carry

    lax.fori_loop(1, n_user, take, 0)

    def sent(d, carry):
        copy(d, me, lax.rem(me + d, n_user)).wait_send()
        return carry

    lax.fori_loop(1, n_user, sent, 0)


def product_kernel(shift, table_ref, items_ref, times_ref, blocks_ref, part_ref, tensor, spread, acc, sem):
    rank = items_ref.shape[2]
    load = pltpu.make_async_copy(blocks_ref, tensor, sem)
    load.start()
    acc[...] = jnp.zeros_like(acc)

    def widen(tile, carry):
        at = pl.multiple_of(tile * BS, BS)
        for s in range(2):
            rows = items_ref[s, pl.ds(at, BS)].astype(jnp.float32)
            for j in range(BS):
                wide = jnp.broadcast_to(rows[j : j + 1], (BS, rank))
                spread[s, tile, j * BS : (j + 1) * BS] = wide.astype(jnp.bfloat16)
        return carry

    lax.fori_loop(0, items_ref.shape[1] // BS, widen, 0)
    load.wait()
    count = table_ref[WIDTH + 1, 0]

    def turn(g, carry):
        for v in range(UNROLL):
            c = g * UNROLL + v
            key = table_ref[WIDTH, c]
            tile = key >> shift
            at = pl.multiple_of((key & ((1 << shift) - 1)) * BS, BS)
            member = [table_ref[m, c] for m in range(WIDTH)]
            x = jnp.concatenate([tensor[word >> 4] for word in member], axis=0)
            for s in range(2):
                right = times_ref[s, pl.ds(at, BS)]
                left = spread[s, tile].reshape(BS, BS, rank)
                khatri = (left * right[None]).reshape(BS * BS, rank)
                y = jnp.dot(x, khatri, preferred_element_type=jnp.float32)
                for m, word in enumerate(member):
                    acc[s, word & 15] += y[m * BS : (m + 1) * BS]
        return carry

    lax.fori_loop(0, (count + UNROLL - 1) // UNROLL, turn, 0)
    tiles = U_DEV // BS
    for half in range(part_ref.shape[0]):
        for s in range(2):
            for n in range(tiles):
                part_ref[half, s, n * BS : (n + 1) * BS] = acc[s, 1 + half * tiles + n]


def gram(rows):
    return lax.dot_general(rows, rows, (((0,), (0,)), ((), ())), preferred_element_type=jnp.float32)


def finish_kernel(part_ref, items_ref, times_ref, rows_ref, grams_ref, theirs, items, send_sem, recv_sem):
    me = lax.axis_index("item")
    other = 1 - me
    barrier = pltpu.get_barrier_semaphore()
    pl.semaphore_signal(barrier, inc=1, device_id={"item": other}, device_id_type=pl.DeviceIdType.MESH)
    pl.semaphore_wait(barrier, 1)
    copies = []
    for n, (src, dst) in enumerate(((part_ref.at[other], theirs), (items_ref, items))):
        copies.append(
            pltpu.make_async_remote_copy(
                src_ref=src, dst_ref=dst, send_sem=send_sem.at[n], recv_sem=recv_sem.at[n],
                device_id={"item": other}, device_id_type=pl.DeviceIdType.MESH,
            )
        )
        copies[-1].start()
    mine = [gram(items_ref[s]) for s in range(2)]
    times = [gram(times_ref[s]) for s in range(2)]
    copies[0].wait()
    rows_ref[...] = part_ref[me] + theirs[...]
    copies[1].wait()
    for s in range(2):
        grams_ref[s] = (mine[s] + gram(items[s])) * times[s]


def local(
    n_user, n_item, blocks, user_blocks, item_blocks, time_blocks, block_counts,
    item_factor, item_previous, time_factor, time_previous,
):
    slots, _, width = blocks.shape
    rank = item_factor.shape[1]
    rows_i, rows_t = item_factor.shape[0], time_factor.shape[0]
    range_tiles = U_DEV * n_item // BS
    per_shard = rows_i // BS
    shift = (rows_t * n_user // BS - 1).bit_length()
    user_local = user_blocks - lax.axis_index("user") * range_tiles
    item_local = item_blocks // per_shard // n_item * per_shard + item_blocks % per_shard
    at = jnp.arange(slots, dtype=jnp.int32)
    key = jnp.where(at < block_counts[0], (item_local << shift) + time_blocks, DEAD)
    size = -(-(slots + UNROLL) // LANE) * LANE
    pad = ((0, size - slots),)
    key = jnp.pad(key, pad, constant_values=DEAD)[None]
    value = jnp.pad(at * 16 + user_local + 1, pad)[None]
    vmem = pl.BlockSpec(memory_space=pltpu.VMEM)
    smem = pl.BlockSpec(memory_space=pltpu.SMEM)
    block_rows = 2 * (rows_i + rows_t)
    items, times, table = pl.pallas_call(
        functools.partial(gather_kernel, n_user),
        out_shape=(
            jax.ShapeDtypeStruct((2, rows_i * n_user, rank), jnp.bfloat16),
            jax.ShapeDtypeStruct((2, rows_t * n_user, rank), jnp.bfloat16),
            jax.ShapeDtypeStruct((8, size), jnp.int32),
        ),
        in_specs=[vmem] * 6,
        out_specs=(vmem, vmem, vmem),
        scratch_shapes=[
            pltpu.VMEM((block_rows, rank), jnp.bfloat16),
            pltpu.VMEM((n_user, block_rows, rank), jnp.bfloat16),
            pltpu.SemaphoreType.DMA((n_user,)),
            pltpu.SemaphoreType.DMA((n_user,)),
        ],
        compiler_params=pltpu.CompilerParams(
            collective_id=0, has_side_effects=True, vmem_limit_bytes=32 << 20
        ),
        name="gather",
    )(key, value, item_factor, item_previous, time_factor, time_previous)
    part = pl.pallas_call(
        functools.partial(product_kernel, shift),
        out_shape=jax.ShapeDtypeStruct((n_item, 2, U_DEV, rank), jnp.float32),
        in_specs=[smem, vmem, vmem, pl.BlockSpec(memory_space=pl.ANY)],
        out_specs=vmem,
        scratch_shapes=[
            pltpu.VMEM(blocks.shape, jnp.bfloat16),
            pltpu.VMEM((2, rows_i * n_user // BS, BS * BS, rank), jnp.bfloat16),
            pltpu.VMEM((2, range_tiles + 1, BS, rank), jnp.float32),
            pltpu.SemaphoreType.DMA,
        ],
        compiler_params=pltpu.CompilerParams(vmem_limit_bytes=48 << 20),
        name="products",
    )(table, items, times, blocks)
    return pl.pallas_call(
        finish_kernel,
        out_shape=(
            jax.ShapeDtypeStruct((2, U_DEV, rank), jnp.float32),
            jax.ShapeDtypeStruct((2, rank, rank), jnp.float32),
        ),
        in_specs=[vmem] * 3,
        out_specs=(vmem, vmem),
        scratch_shapes=[
            pltpu.VMEM((2, U_DEV, rank), jnp.float32),
            pltpu.VMEM((2, rows_i * n_user, rank), jnp.bfloat16),
            pltpu.SemaphoreType.DMA((2,)),
            pltpu.SemaphoreType.DMA((2,)),
        ],
        compiler_params=pltpu.CompilerParams(
            collective_id=1, has_side_effects=True, vmem_limit_bytes=32 << 20
        ),
        name="finish",
    )(part, items, times)


def solution(mesh):
    in_specs = (
        P(("groups", "user", "item"), None, None),
        P(("groups", "user", "item")),
        P(("groups", "user", "item")),
        P(("groups", "user", "item")),
        P(("groups", "user", "item")),
        P(("groups", "user", "item"), None),
        P(("groups", "user", "item"), None),
        P(("groups", "user"), None),
        P(("groups", "user"), None),
    )
    out_specs = (P(None, ("groups", "user", "item"), None), P("groups", None, None))
    body = functools.partial(local, mesh.shape["user"], mesh.shape["item"])
    return jax.shard_map(body, mesh=mesh, in_specs=in_specs, out_specs=out_specs, check_vma=False)
```

time: 331 us -> 49.7 us (0.15)
  the two profiles are of different devices: /device:TPU:0 before, /device:TPU:31 now
where the time goes in v1:
time: 49.7 us; the launch traced here: 49.6 us
  Pallas kernels  40.6 us (82%)
  local copies, waits for them, and re-layouts  6.28 us (13%)
  other arithmetic  1.4 us (3%)
  between operations  1.33 us (3%)
    pallas_call x1, Pallas kernels, local(): pl.pallas_call(functools.partial(gather_kernel, n_user), out_shape=(jax.S...  15.6 us
    pallas_call x1, Pallas kernels, local(): pl.pallas_call(functools.partial(product_kernel, shift), out_shape=jax.Sh...  14.7 us
    pallas_call x1, Pallas kernels, local(): pl.pallas_call(finish_kernel, out_shape=(jax.ShapeDtypeStruct((2, U_DEV,...  10.2 us
    unnamed x12, local copies, waits for them, and re-layouts  6.26 us

profile of v1, /device:TPU:31, one launch (start us, length us, event | category | flops | bytes accessed | tf_op | source)
XLA Modules:
  0.0 49.6 jit_solution(3608716307713117432)
XLA Ops:
  1.3 0.7 %add_add_fusion = s32[448]{0:T(512)S(1)} fusion(s32[448]{0:T(512)} %param.10, s32[]{:T(128)S(6)} %mul.11), kind=kLoop, calls=%fused_computation.8 | loop fusion | flops 1792 | bytes 3588 | tf_op jit(solution)/shard_map/add | solution.py:219
  2.0 0.7 %fusion.3 = s32[448]{0:T(512)S(1)} fusion(s32[448]{0:T(512)} %param.12, s32[448]{0:T(512)} %param.11, s32[]{:T(128)} %bitcast.3), kind=kLoop, calls=%fused_computation.7 | loop fusion | flops 8512 | bytes 5380 | tf_op jit(solution)/shard_map/jit(_where)/select_n | solution.py:215
  2.7 0.0 copy-start.1
  2.7 0.7 %copy-done.1 = bf16[16,256]{1,0:T(8,128)(2,1)S(1)} copy-done((bf16[16,256]{1,0:T(8,128)(2,1)S(1)}, bf16[16,256]{1,0:T(8,128)(2,1)}, u32[]{:S(2)}) %copy-start.1) | copy-done | bytes 8216
  3.4 0.0 copy-start.2
  3.4 0.7 %copy-done.2 = bf16[16,256]{1,0:T(8,128)(2,1)S(1)} copy-done((bf16[16,256]{1,0:T(8,128)(2,1)S(1)}, bf16[16,256]{1,0:T(8,128)(2,1)}, u32[]{:S(2)}) %copy-start.2) | copy-done | bytes 8216
  4.1 0.0 copy-start.3
  4.1 0.7 %copy-done.3 = bf16[16,256]{1,0:T(8,128)(2,1)S(1)} copy-done((bf16[16,256]{1,0:T(8,128)(2,1)S(1)}, bf16[16,256]{1,0:T(8,128)(2,1)}, u32[]{:S(2)}) %copy-start.3) | copy-done | bytes 8216
  4.8 0.0 copy-start.4
  4.8 0.7 %copy-done.4 = bf16[16,256]{1,0:T(8,128)(2,1)S(1)} copy-done((bf16[16,256]{1,0:T(8,128)(2,1)S(1)}, bf16[16,256]{1,0:T(8,128)(2,1)}, u32[]{:S(2)}) %copy-start.4) | copy-done | bytes 8216
  5.5 15.6 %gather.1 = (bf16[2,256,256]{2,1,0:T(8,128)(2,1)S(1)}, bf16[2,256,256]{2,1,0:T(8,128)(2,1)S(1)}, s32[8,512]{1,0:T(8,128)S(1)}) custom-call(s32[1,512]{1,0:T(1,128)S(1)} %bitcast.5, s32[1,512]{1,0:T(1,128)S(1)} %bitcast.4, bf16[16,256]{1,0:T(8,128)(2,1)S(1)} %copy-done.1, bf16[16,256]{1,0:T(8,128)(2,1)S(1)} %copy-done.2, bf16[16,256]{1,0:T(8,128)(2,1)S(1)} %copy-done.3, ...), custom_call_target="tpu_custom_call" | custom-call | tf_op jit(solution)/shard_map/gather/pallas_call | solution.py:223
  21.1 0.0 copy-start
  21.1 2.0 %copy-done = bf16[448,16,256]{2,1,0:T(8,128)(2,1)S(1)} copy-done((bf16[448,16,256]{2,1,0:T(8,128)(2,1)S(1)}, bf16[448,16,256]{2,1,0:T(8,128)(2,1)}, u32[]{:S(2)}) %copy-start) | copy-done | bytes 3670040
  23.2 14.7 %products.1.part_ref = f32[2,2,64,256]{3,2,1,0:T(8,128)S(1)} custom-call(s32[8,512]{1,0:T(8,128)S(1)} %get-tuple-element.5.table_ref, bf16[2,256,256]{2,1,0:T(8,128)(2,1)S(1)} %get-tuple-element.6.items_ref, bf16[2,256,256]{2,1,0:T(8,128)(2,1)S(1)} %get-tuple-element.7.times_ref, bf16[448,16,256]{2,1,0:T(8,128)(2,1)S(1)} %copy-done), custom_call_target="tpu_custom_call" | custom-call | tf_op jit(solution)/shard_map/products/pallas_call | solution.py:243
  37.9 10.2 %finish.1 = (f32[2,64,256]{2,1,0:T(8,128)S(1)}, f32[2,256,256]{2,1,0:T(8,128)S(1)}) custom-call(f32[2,2,64,256]{3,2,1,0:T(8,128)S(1)} %products.1.part_ref, bf16[2,256,256]{2,1,0:T(8,128)(2,1)S(1)} %get-tuple-element.6.items_ref, bf16[2,256,256]{2,1,0:T(8,128)(2,1)S(1)} %get-tuple-element.7.times_ref), custom_call_target="tpu_custom_call" | custom-call | tf_op jit(solution)/shard_map/finish/pallas_call | solution.py:257
  48.1 0.7 %copy.14 = f32[2,64,256]{2,1,0:T(8,128)} copy(f32[2,64,256]{2,1,0:T(8,128)S(1)} %get-tuple-element.10) | data formatting | bytes 262144
  48.8 0.8 %copy.15 = f32[2,256,256]{2,1,0:T(8,128)} copy(f32[2,256,256]{2,1,0:T(8,128)S(1)} %get-tuple-element.11) | data formatting | bytes 1048576
  (2 shorter events, 0.0 us)
Async XLA Ops:
  2.7 0.7 %copy-start.1 = (bf16[16,256]{1,0:T(8,128)(2,1)S(1)}, bf16[16,256]{1,0:T(8,128)(2,1)}, u32[]{:S(2)}) copy-start(bf16[16,256]{1,0:T(8,128)(2,1)} %item_ref.1) | copy-start | bytes 24580
  3.4 0.7 %copy-start.2 = (bf16[16,256]{1,0:T(8,128)(2,1)S(1)}, bf16[16,256]{1,0:T(8,128)(2,1)}, u32[]{:S(2)}) copy-start(bf16[16,256]{1,0:T(8,128)(2,1)} %item_old_ref.1) | copy-start | bytes 24580
  4.1 0.7 %copy-start.3 = (bf16[16,256]{1,0:T(8,128)(2,1)S(1)}, bf16[16,256]{1,0:T(8,128)(2,1)}, u32[]{:S(2)}) copy-start(bf16[16,256]{1,0:T(8,128)(2,1)} %time_ref.1) | copy-start | bytes 24580
  4.8 0.7 %copy-start.4 = (bf16[16,256]{1,0:T(8,128)(2,1)S(1)}, bf16[16,256]{1,0:T(8,128)(2,1)}, u32[]{:S(2)}) copy-start(bf16[16,256]{1,0:T(8,128)(2,1)} %time_old_ref.1) | copy-start | bytes 24580
  21.1 2.0 %copy-start = (bf16[448,16,256]{2,1,0:T(8,128)(2,1)S(1)}, bf16[448,16,256]{2,1,0:T(8,128)(2,1)}, u32[]{:S(2)}) copy-start(bf16[448,16,256]{2,1,0:T(8,128)(2,1)} %blocks_ref.1) | copy-start | bytes 11010052

commit v2 on v1

--- a/solution.py
+++ b/solution.py
@@ -11,8 +11,9 @@
 U_DEV = 64
 LANE = 128
 WIDTH = 4
-UNROLL = 4
-DEAD = 1 << 28
+UNROLL = 16
+SHIFT = 13
+PLANE = 4
 
 extrapolation = 0.5
 
@@ -31,106 +32,171 @@
     return jnp.concatenate(parts, axis=0)
 
 
-def plan_groups(key, value, table_ref):
-    size = key.shape[1]
+def order_slots(word, size):
     down = lax.broadcasted_iota(jnp.int32, (size, LANE), 0)
     across = lax.broadcasted_iota(jnp.int32, (1, LANE), 1)
-    chunks = [slice(at, at + LANE) for at in range(0, size, LANE)]
+    key = word >> SHIFT
     key_col = as_columns(key, size)
     places = []
-    for n, cut in enumerate(chunks):
-        earlier = (key_col == key[:, cut]) & (down < across + n * LANE)
+    for at in range(0, size, LANE):
+        earlier = (key_col == key[:, at : at + LANE]) & (down < across + at)
         places.append(jnp.sum(earlier.astype(jnp.int32), axis=0, keepdims=True))
     place = jnp.concatenate(places, axis=1)
-    alive = key < DEAD
-    order = jnp.where(alive, key * size + place, jnp.int32(2**31 - 1))
+    return jnp.where(word >= 0, key * size + place, jnp.int32(2**31 - 1)), place
+
+
+def group_slots(word, order, place, size):
     order_col = as_columns(order, size)
     leads = (order_col & (WIDTH - 1)) == 0
     groups = []
-    for cut in chunks:
-        ahead = leads & (order_col <= order[:, cut])
+    for at in range(0, size, LANE):
+        ahead = leads & (order_col <= order[:, at : at + LANE])
         groups.append(jnp.sum(ahead.astype(jnp.int32), axis=0, keepdims=True))
     group = jnp.concatenate(groups, axis=1) - 1
-    spot = jnp.where(alive, group * WIDTH + (place & (WIDTH - 1)), -1)
+    spot = jnp.where(word >= 0, group * WIDTH + (place & (WIDTH - 1)), -1)
+    return spot, jnp.sum(leads.astype(jnp.int32), axis=0, keepdims=True)
+
+
+def fill_table(word, spot, total, table_ref, size):
+    across = lax.broadcasted_iota(jnp.int32, (1, LANE), 1)
     spot_col = as_columns(spot, size)
-    value_col = as_columns(value, size)
-    zero = jnp.zeros_like(key_col)
+    word_col = as_columns(word, size)
+    zero = jnp.zeros_like(word_col)
     table_ref[...] = jnp.zeros(table_ref.shape, jnp.int32)
-    for n, cut in enumerate(chunks):
-        base = (across + n * LANE) * WIDTH
+    for at in range(0, size, LANE):
         for m in range(WIDTH):
-            here = spot_col == base + m
-            picked = jnp.sum(jnp.where(here, value_col, zero), axis=0, keepdims=True)
-            table_ref[m : m + 1, cut] = picked
-            if m == 0:
-                keys = jnp.sum(jnp.where(here, key_col, zero), axis=0, keepdims=True)
-                table_ref[WIDTH : WIDTH + 1, cut] = keys
-    total = jnp.sum(leads.astype(jnp.int32), axis=0, keepdims=True)
-    table_ref[WIDTH + 1 : WIDTH + 2, 0:LANE] = total
+            here = spot_col == (across + at) * WIDTH + m
+            picked = jnp.sum(jnp.where(here, word_col, zero), axis=0, keepdims=True)
+            table_ref[m : m + 1, at : at + LANE] = picked
+    table_ref[WIDTH : WIDTH + 1, 0:LANE] = total
+
+
+def flip(index, bits):
+    bit = 1
+    while bit <= bits:
+        if bits & bit:
+            index = index + bit - 2 * bit * ((index // bit) % 2)
+        bit *= 2
+    return index
 
 
 def gather_kernel(
-    n_user, key_ref, value_ref, item_ref, item_old_ref, time_ref, time_old_ref,
-    items_ref, times_ref, table_ref, own, held, send_sem, recv_sem,
+    n_user, plane, word_ref, item_hbm, item_old_hbm, time_hbm, time_old_hbm,
+    items_ref, times_ref, table_ref, item_ref, item_old_ref, time_ref, time_old_ref, own, held, crossed,
+    load_sem, line_send, plane_send, cross_send, recv, cross_recv,
 ):
-    me = lax.axis_index("user")
+    lines = n_user // plane
+    me, core = lax.axis_index("user"), lax.axis_index("item")
+    line, spot = me // plane, me % plane
     rows_i, rows_t = item_ref.shape[0], time_ref.shape[0]
+    loads = [
+        pltpu.make_async_copy(src, dst, load_sem.at[n])
+        for n, (src, dst) in enumerate(
+            ((item_hbm, item_ref), (item_old_hbm, item_old_ref), (time_hbm, time_ref), (time_old_hbm, time_old_ref))
+        )
+    ]
+    for load in loads:
+        load.start()
     barrier = pltpu.get_barrier_semaphore()
 
-    def greet(d, carry):
-        peer = lax.rem(me + d, n_user)
-        pl.semaphore_signal(barrier, inc=1, device_id={"user": peer}, device_id_type=pl.DeviceIdType.MESH)
-        return carry
-
-    lax.fori_loop(1, n_user, greet, 0)
-    own[0:rows_i] = item_ref[...]
-    own[rows_i : 2 * rows_i] = extended(item_ref[...], item_old_ref[...])
-    own[2 * rows_i : 2 * rows_i + rows_t] = time_ref[...]
-    own[2 * rows_i + rows_t :] = extended(time_ref[...], time_old_ref[...])
-    pl.semaphore_wait(barrier, n_user - 1)
-
-    def copy(d, slot, peer):
+    def to(user):
+        return {"user": user}
+
+    line_peers = [flip(line, d) * plane + spot for d in range(1, lines)]
+    plane_peers = [line * plane + flip(spot, d) for d in range(1, plane)]
+    for peer in line_peers + plane_peers:
+        pl.semaphore_signal(barrier, inc=1, device_id=to(peer), device_id_type=pl.DeviceIdType.MESH)
+    pl.semaphore_signal(barrier, inc=1, device_id={"item": 1 - core}, device_id_type=pl.DeviceIdType.MESH)
+    for load in loads:
+        load.wait()
+    item, time = item_ref[...], time_ref[...]
+    item_new, time_new = extended(item, item_old_ref[...]), extended(time, time_old_ref[...])
+    own[0:rows_i] = item
+    own[rows_i : 2 * rows_i] = item_new
+    first = jnp.broadcast_to(core, time.shape) == 0
+    own[2 * rows_i :] = jnp.where(first, time.astype(jnp.float32), time_new.astype(jnp.float32)).astype(jnp.bfloat16)
+    pl.semaphore_wait(barrier, lines + plane - 1)
+
+    def copy(src, dst, send, receive, device):
         return pltpu.make_async_remote_copy(
-            src_ref=own, dst_ref=held.at[slot], send_sem=send_sem.at[d], recv_sem=recv_sem.at[d],
-            device_id={"user": peer}, device_id_type=pl.DeviceIdType.MESH,
+            src_ref=src, dst_ref=dst, send_sem=send, recv_sem=receive,
+            device_id=device, device_id_type=pl.DeviceIdType.MESH,
         )
 
-    def send(d, carry):
-        copy(d, me, lax.rem(me + d, n_user)).start()
-        return carry
-
-    lax.fori_loop(1, n_user, send, 0)
-    plan_groups(key_ref[...], value_ref[...], table_ref)
-
-    def place(source, block):
+    sends = []
+    for d in range(1, lines):
+        sends.append(copy(own, held.at[me], line_send.at[d], recv.at[me], to(line_peers[d - 1])))
+    for d in range(1, plane):
+        sends.append(copy(own, held.at[me], plane_send.at[0, d], recv.at[me], to(plane_peers[d - 1])))
+    for send in sends:
+        send.start()
+
+    def arrive(source):
+        copy(held.at[source], held.at[source], line_send.at[0], recv.at[source], to(source)).wait_recv()
+
+    def across(source, n):
+        return copy(
+            held.at[source, pl.ds(2 * rows_i, rows_t)], crossed.at[source],
+            cross_send.at[n], cross_recv.at[source], {"item": 1 - core},
+        )
+
+    def forward(d):
+        source = line_peers[d - 1]
+        arrive(source)
+        for e in range(1, plane):
+            sends.append(copy(held.at[source], held.at[source], plane_send.at[d, e], recv.at[source], to(plane_peers[e - 1])))
+            sends[-1].start()
+        sends.append(across(source, d * plane))
+        sends[-1].start()
+
+    size = word_ref.shape[1]
+    word = word_ref[...]
+    order, place = order_slots(word, size)
+    if lines > 1:
+        forward(1)
+    slot, total = group_slots(word, order, place, size)
+    for d in range(2, lines):
+        forward(d)
+    fill_table(word, slot, total, table_ref, size)
+
+    def put(source, block):
         at_i = pl.multiple_of(source * rows_i, rows_i)
         at_t = pl.multiple_of(source * rows_t, rows_t)
         for s in range(2):
             items_ref[s, pl.ds(at_i, rows_i)] = block[s * rows_i : (s + 1) * rows_i]
-            low = 2 * rows_i + s * rows_t
-            times_ref[s, pl.ds(at_t, rows_t)] = block[low : low + rows_t]
-
-    place(me, own)
-
-    def take(d, carry):
-        source = lax.rem(me - d + n_user, n_user)
-        copy(d, source, source).wait_recv()
-        place(source, held.at[source])
-        return carry
-
-    lax.fori_loop(1, n_user, take, 0)
-
-    def sent(d, carry):
-        copy(d, me, lax.rem(me + d, n_user)).wait_send()
-        return carry
-
-    lax.fori_loop(1, n_user, sent, 0)
-
-
-def product_kernel(shift, table_ref, items_ref, times_ref, blocks_ref, part_ref, tensor, spread, acc, sem):
+        times_ref[core, pl.ds(at_t, rows_t)] = block[2 * rows_i :]
+
+    at_me = pl.multiple_of(me * rows_t, rows_t)
+    times_ref[0, pl.ds(at_me, rows_t)] = time
+    times_ref[1, pl.ds(at_me, rows_t)] = time_new
+    for s, rows in enumerate((item, item_new)):
+        items_ref[s, pl.ds(pl.multiple_of(me * rows_i, rows_i), rows_i)] = rows
+    sources = [(d * plane, line_peers[d - 1]) for d in range(1, lines)]
+    for d in range(lines):
+        for e in range(1, plane):
+            source = flip(line, d) * plane + flip(spot, e)
+            arrive(source)
+            sends.append(across(source, d * plane + e))
+            sends[-1].start()
+            sources.append((d * plane + e, source))
+    for n, source in sources:
+        put(source, held.at[source])
+    for n, source in sources:
+        across(source, n).wait_recv()
+        at_t = pl.multiple_of(source * rows_t, rows_t)
+        times_ref[1 - core, pl.ds(at_t, rows_t)] = crossed[source]
+    for send in sends:
+        send.wait_send()
+
+
+def product_kernel(
+    shift, table_hbm, items_ref, times_ref, blocks_ref, part_ref, tensor, spread, acc, table_ref, sem, table_sem
+):
     rank = items_ref.shape[2]
     load = pltpu.make_async_copy(blocks_ref, tensor, sem)
     load.start()
+    plan = pltpu.make_async_copy(table_hbm, table_ref, table_sem)
+    plan.start()
     acc[...] = jnp.zeros_like(acc)
 
     def widen(tile, carry):
@@ -143,17 +209,18 @@
         return carry
 
     lax.fori_loop(0, items_ref.shape[1] // BS, widen, 0)
+    plan.wait()
     load.wait()
-    count = table_ref[WIDTH + 1, 0]
+    count = table_ref[WIDTH, 0]
 
     def turn(g, carry):
         for v in range(UNROLL):
             c = g * UNROLL + v
-            key = table_ref[WIDTH, c]
+            member = [table_ref[m, c] for m in range(WIDTH)]
+            key = member[0] >> SHIFT
             tile = key >> shift
             at = pl.multiple_of((key & ((1 << shift) - 1)) * BS, BS)
-            member = [table_ref[m, c] for m in range(WIDTH)]
-            x = jnp.concatenate([tensor[word >> 4] for word in member], axis=0)
+            x = jnp.concatenate([tensor[(word >> 4) & 511] for word in member], axis=0)
             for s in range(2):
                 right = times_ref[s, pl.ds(at, BS)]
                 left = spread[s, tile].reshape(BS, BS, rank)
@@ -212,44 +279,56 @@
     user_local = user_blocks - lax.axis_index("user") * range_tiles
     item_local = item_blocks // per_shard // n_item * per_shard + item_blocks % per_shard
     at = jnp.arange(slots, dtype=jnp.int32)
-    key = jnp.where(at < block_counts[0], (item_local << shift) + time_blocks, DEAD)
+    word = (((item_local << shift) + time_blocks) << SHIFT) + at * 16 + user_local + 1
+    word = jnp.where(at < block_counts[0], word, -1)
     size = -(-(slots + UNROLL) // LANE) * LANE
-    pad = ((0, size - slots),)
-    key = jnp.pad(key, pad, constant_values=DEAD)[None]
-    value = jnp.pad(at * 16 + user_local + 1, pad)[None]
+    word = jnp.pad(word, ((0, size - slots),), constant_values=-1)[None]
     vmem = pl.BlockSpec(memory_space=pltpu.VMEM)
-    smem = pl.BlockSpec(memory_space=pltpu.SMEM)
-    block_rows = 2 * (rows_i + rows_t)
+    hbm = pl.BlockSpec(memory_space=pl.ANY)
+    plane = PLANE if n_user % PLANE == 0 else 1
+    block_rows = 2 * rows_i + rows_t
+    dma = pltpu.SemaphoreType.DMA
     items, times, table = pl.pallas_call(
-        functools.partial(gather_kernel, n_user),
+        functools.partial(gather_kernel, n_user, plane),
         out_shape=(
             jax.ShapeDtypeStruct((2, rows_i * n_user, rank), jnp.bfloat16),
             jax.ShapeDtypeStruct((2, rows_t * n_user, rank), jnp.bfloat16),
             jax.ShapeDtypeStruct((8, size), jnp.int32),
         ),
-        in_specs=[vmem] * 6,
+        in_specs=[vmem] + [hbm] * 4,
         out_specs=(vmem, vmem, vmem),
         scratch_shapes=[
+            pltpu.VMEM((rows_i, rank), jnp.bfloat16),
+            pltpu.VMEM((rows_i, rank), jnp.bfloat16),
+            pltpu.VMEM((rows_t, rank), jnp.bfloat16),
+            pltpu.VMEM((rows_t, rank), jnp.bfloat16),
             pltpu.VMEM((block_rows, rank), jnp.bfloat16),
             pltpu.VMEM((n_user, block_rows, rank), jnp.bfloat16),
-            pltpu.SemaphoreType.DMA((n_user,)),
-            pltpu.SemaphoreType.DMA((n_user,)),
+            pltpu.VMEM((n_user, rows_t, rank), jnp.bfloat16),
+            dma((4,)),
+            dma((n_user // plane,)),
+            dma((n_user // plane, plane)),
+            dma((n_user,)),
+            dma((n_user,)),
+            dma((n_user,)),
         ],
         compiler_params=pltpu.CompilerParams(
             collective_id=0, has_side_effects=True, vmem_limit_bytes=32 << 20
         ),
         name="gather",
-    )(key, value, item_factor, item_previous, time_factor, time_previous)
+    )(word, item_factor, item_previous, time_factor, time_previous)
     part = pl.pallas_call(
         functools.partial(product_kernel, shift),
         out_shape=jax.ShapeDtypeStruct((n_item, 2, U_DEV, rank), jnp.float32),
-        in_specs=[smem, vmem, vmem, pl.BlockSpec(memory_space=pl.ANY)],
+        in_specs=[hbm, vmem, vmem, hbm],
         out_specs=vmem,
         scratch_shapes=[
             pltpu.VMEM(blocks.shape, jnp.bfloat16),
             pltpu.VMEM((2, rows_i * n_user // BS, BS * BS, rank), jnp.bfloat16),
             pltpu.VMEM((2, range_tiles + 1, BS, rank), jnp.float32),
-            pltpu.SemaphoreType.DMA,
+            pltpu.SMEM((8, size), jnp.int32),
+            dma,
+            dma,
         ],
         compiler_params=pltpu.CompilerParams(vmem_limit_bytes=48 << 20),
         name="products",

time: 49.7 us -> 39.7 us (0.80)
  the two profiles are of different devices: /device:TPU:31 before, /device:TPU:5 now
where the time goes in v2:
time: 39.7 us; the launch traced here: 39.9 us
  Pallas kernels  31.6 us (80%)
  local copies, waits for them, and re-layouts  6.27 us (16%)
  between operations  1.33 us (3%)
  other arithmetic  0.73 us (2%)
    pallas_call x1, Pallas kernels, local(): pl.pallas_call(functools.partial(product_kernel, shift), out_shape=jax.Sh...  15.9 us
    pallas_call x1, Pallas kernels, local(): pl.pallas_call(functools.partial(gather_kernel, n_user, plane), out_shape...  13.6 us
    unnamed x12, local copies, waits for them, and re-layouts  6.27 us
    pallas_call x1, Pallas kernels, local(): pl.pallas_call(finish_kernel, out_shape=(jax.ShapeDtypeStruct((2, U_DEV,...  2.12 us

profile of v2, /device:TPU:5, one launch (start us, length us, event | category | flops | bytes accessed | tf_op | source)
XLA Modules:
  0.0 39.9 jit_solution(12055770060665343531)
XLA Ops:
  1.3 0.7 %add_select_fusion.1 = s32[448]{0:T(512)S(1)} fusion(s32[448]{0:T(512)} %param.10, s32[448]{0:T(512)} %param.12, s32[448]{0:T(512)} %param.11, s32[]{:T(128)S(6)} %mul.11, s32[]{:T(128)} %bitcast.2), kind=kLoop, calls=%fused_computation.10 | loop fusion | flops 11200 | bytes 7176 | tf_op jit(solution)/shard_map/jit(_where)/select_n | solution.py:283
  2.0 0.0 copy-start.1
  2.0 0.7 %copy-done.1 = bf16[16,256]{1,0:T(8,128)(2,1)S(1)} copy-done((bf16[16,256]{1,0:T(8,128)(2,1)S(1)}, bf16[16,256]{1,0:T(8,128)(2,1)}, u32[]{:S(2)}) %copy-start.1) | copy-done | bytes 8216
  2.7 0.0 copy-start.2
  2.7 0.7 %copy-done.2 = bf16[16,256]{1,0:T(8,128)(2,1)S(1)} copy-done((bf16[16,256]{1,0:T(8,128)(2,1)S(1)}, bf16[16,256]{1,0:T(8,128)(2,1)}, u32[]{:S(2)}) %copy-start.2) | copy-done | bytes 8216
  3.4 0.0 copy-start.3
  3.4 0.7 %copy-done.3 = bf16[16,256]{1,0:T(8,128)(2,1)S(1)} copy-done((bf16[16,256]{1,0:T(8,128)(2,1)S(1)}, bf16[16,256]{1,0:T(8,128)(2,1)}, u32[]{:S(2)}) %copy-start.3) | copy-done | bytes 8216
  4.1 0.0 copy-start.4
  4.1 0.7 %copy-done.4 = bf16[16,256]{1,0:T(8,128)(2,1)S(1)} copy-done((bf16[16,256]{1,0:T(8,128)(2,1)S(1)}, bf16[16,256]{1,0:T(8,128)(2,1)}, u32[]{:S(2)}) %copy-start.4) | copy-done | bytes 8216
  4.8 13.6 %gather.1 = (bf16[2,256,256]{2,1,0:T(8,128)(2,1)S(1)}, bf16[2,256,256]{2,1,0:T(8,128)(2,1)S(1)}, s32[8,512]{1,0:T(8,128)S(1)}) custom-call(s32[1,512]{1,0:T(1,128)S(1)} %bitcast.3, bf16[16,256]{1,0:T(8,128)(2,1)S(1)} %copy-done.1, bf16[16,256]{1,0:T(8,128)(2,1)S(1)} %copy-done.2, bf16[16,256]{1,0:T(8,128)(2,1)S(1)} %copy-done.3, bf16[16,256]{1,0:T(8,128)(2,1)S(1)} %copy-done.4), custom_call_target="tpu_custom_call" | custom-call | tf_op jit(solution)/shard_map/gather/pallas_call | solution.py:291
  18.4 0.0 copy-start
  18.4 2.0 %copy-done = bf16[448,16,256]{2,1,0:T(8,128)(2,1)S(1)} copy-done((bf16[448,16,256]{2,1,0:T(8,128)(2,1)S(1)}, bf16[448,16,256]{2,1,0:T(8,128)(2,1)}, u32[]{:S(2)}) %copy-start) | copy-done | bytes 3670040
  20.5 15.9 %products.1.part_ref = f32[2,2,64,256]{3,2,1,0:T(8,128)S(1)} custom-call(s32[8,512]{1,0:T(8,128)S(1)} %get-tuple-element.5.table_hbm, bf16[2,256,256]{2,1,0:T(8,128)(2,1)S(1)} %get-tuple-element.6.items_ref, bf16[2,256,256]{2,1,0:T(8,128)(2,1)S(1)} %get-tuple-element.7.times_ref, bf16[448,16,256]{2,1,0:T(8,128)(2,1)S(1)} %copy-done), custom_call_target="tpu_custom_call" | custom-call | tf_op jit(solution)/shard_map/products/pallas_call | solution.py:320
  36.4 2.1 %finish.1 = (f32[2,64,256]{2,1,0:T(8,128)S(1)}, f32[2,256,256]{2,1,0:T(8,128)S(1)}) custom-call(f32[2,2,64,256]{3,2,1,0:T(8,128)S(1)} %products.1.part_ref, bf16[2,256,256]{2,1,0:T(8,128)(2,1)S(1)} %get-tuple-element.6.items_ref, bf16[2,256,256]{2,1,0:T(8,128)(2,1)S(1)} %get-tuple-element.7.times_ref), custom_call_target="tpu_custom_call" | custom-call | tf_op jit(solution)/shard_map/finish/pallas_call | solution.py:336
  38.5 0.7 %copy.14 = f32[2,64,256]{2,1,0:T(8,128)} copy(f32[2,64,256]{2,1,0:T(8,128)S(1)} %get-tuple-element.10) | data formatting | bytes 262144
  39.1 0.8 %copy.15 = f32[2,256,256]{2,1,0:T(8,128)} copy(f32[2,256,256]{2,1,0:T(8,128)S(1)} %get-tuple-element.11) | data formatting | bytes 1048576
  (1 shorter events, 0.0 us)
Async XLA Ops:
  2.0 0.7 %copy-start.1 = (bf16[16,256]{1,0:T(8,128)(2,1)S(1)}, bf16[16,256]{1,0:T(8,128)(2,1)}, u32[]{:S(2)}) copy-start(bf16[16,256]{1,0:T(8,128)(2,1)} %item_hbm.1) | copy-start | bytes 24580
  2.7 0.7 %copy-start.2 = (bf16[16,256]{1,0:T(8,128)(2,1)S(1)}, bf16[16,256]{1,0:T(8,128)(2,1)}, u32[]{:S(2)}) copy-start(bf16[16,256]{1,0:T(8,128)(2,1)} %item_old_hbm.1) | copy-start | bytes 24580
  3.4 0.7 %copy-start.3 = (bf16[16,256]{1,0:T(8,128)(2,1)S(1)}, bf16[16,256]{1,0:T(8,128)(2,1)}, u32[]{:S(2)}) copy-start(bf16[16,256]{1,0:T(8,128)(2,1)} %time_hbm.1) | copy-start | bytes 24580
  4.1 0.7 %copy-start.4 = (bf16[16,256]{1,0:T(8,128)(2,1)S(1)}, bf16[16,256]{1,0:T(8,128)(2,1)}, u32[]{:S(2)}) copy-start(bf16[16,256]{1,0:T(8,128)(2,1)} %time_old_hbm.1) | copy-start | bytes 24580
  18.4 2.0 %copy-start = (bf16[448,16,256]{2,1,0:T(8,128)(2,1)S(1)}, bf16[448,16,256]{2,1,0:T(8,128)(2,1)}, u32[]{:S(2)}) copy-start(bf16[448,16,256]{2,1,0:T(8,128)(2,1)} %blocks_ref.1) | copy-start | bytes 11010052
